TPU v7x, 512 devices: a whole 4x8x8 slice. The times are simulated.
512 devices in a mesh: rep: 16 (over z, core), fsdp: 32 (over y, x).
Axes of the slice: x: 4, y: 8, z: 8, core: 2. Of those that a mesh axis runs over, the one named last changes fastest.
Arguments:
- parent: bfloat16 [1024, 8192], P('fsdp'), may hold values from -6 to 6
- local_weights: bfloat16 [16, 1024, 8192], P('rep', 'fsdp'), may hold values from -6 to 6
- error: float32 [16, 1024, 8192], P('rep', 'fsdp'), may hold values from -4 to 4
- q_start: bfloat16 [8192, 128], P('fsdp'), may hold values from -0.0625 to 0.0625
Outputs:
- update: bfloat16 [1024, 8192], P('fsdp')
- new_error: float32 [16, 1024, 8192], P('rep', 'fsdp')
- new_q: float32 [8192, 128], P('fsdp')
All inputs are finite; a program needn't handle non-finite values.
Results may differ from a plain program's by a relative error of at most 0.022.
Values may be sent and summed in bfloat16 or wider, within the bound.
No kernel may reach another device: no remote copies, remote signals or barrier semaphores. Data moves between devices by JAX's collectives and lax.ppermute only.
A program may use at most 64 MiB of HBM per device.

v0:
```python
import jax
import jax.numpy as jnp
from jax import lax
from jax.sharding import PartitionSpec as P


def column_product(left, right):
    return lax.dot_general(
        left, right, (((0,), (0,)), ((), ())), preferred_element_type=jnp.float32
    )


def per_device(parent, local_weights, error, q_start):
    merged = local_weights[0].astype(jnp.float32) - parent.astype(jnp.float32) + error[0]
    merged_bf = merged.astype(jnp.bfloat16)
    replicas = lax.axis_size("rep")
    columns = merged_bf
    local_p = jnp.dot(
        columns,
        lax.all_gather(q_start, "fsdp", axis=0, tiled=True),
        preferred_element_type=jnp.float32,
    )
    mean_p = lax.psum(local_p, "rep") / replicas
    gram = lax.psum(jnp.dot(mean_p.T, mean_p, precision=lax.Precision.HIGHEST), "fsdp")
    lower = jnp.linalg.cholesky(gram)
    ortho = jax.scipy.linalg.solve_triangular(lower, mean_p.T, lower=True).T
    ortho_bf = ortho.astype(jnp.bfloat16)
    columns = merged_bf
    shard = lax.psum_scatter(
        column_product(columns, ortho_bf), "fsdp", scatter_dimension=0, tiled=True
    )
    new_q = lax.psum(shard, "rep") / replicas
    q_bf = new_q.astype(jnp.bfloat16)
    approx = lax.dot_general(
        ortho_bf,
        lax.all_gather(q_bf, "fsdp", axis=0, tiled=True),
        (((1,), (1,)), ((), ())),
        preferred_element_type=jnp.float32,
    )
    update = approx.astype(jnp.bfloat16)
    new_error = (merged - approx)[None]
    return (update, new_error, new_q)


def solution(mesh):
    placed = (P("fsdp", None), P("rep", "fsdp", None), P("rep", "fsdp", None), P("fsdp", None))
    return jax.shard_map(
        per_device,
        mesh=mesh,
        in_specs=placed,
        out_specs=(P("fsdp", None), P("rep", "fsdp", None), P("fsdp", None)),
        check_vma=False,
    )
```

profile of v0, /device:TPU:1, one launch (start us, length us, event | category | flops | bytes accessed | tf_op | source)
XLA Modules:
  0.0 757.1 jit_solution(1289677410058340171)
XLA Ops:
  7.2 0.0 all-gather.3.cloned.1.call-start
  7.2 0.7 all-gather.3.cloned.1.call-update
  7.9 0.0 all-reduce.3.cloned.1.call-start
  7.9 1.7 fusion.1
  9.6 86.6 %all-gather.3.cloned.1.call-done = bf16[8192,128]{1,0:T(8,128)(2,1)} async-done(((bf16[256,128]{1,0:T(8,128)(2,1)}), bf16[8192,128]{1,0:T(8,128)(2,1)}) %all-gather.3.cloned.1.call-update) | async-done | bytes 2097168 | tf_op jit(solution)/shard_map/all_gather | solution.py:20
  96.2 2.0 fusion.13
  98.3 47.6 %psum.21 = f32[32,128]{1,0:T(8,128)S(1)} all-reduce(f32[32,128]{1,0:T(8,128)S(1)} %fusion.13), channel_id=1, replica_groups=mesh['rep'=16,'fsdp'=32] {'rep'}, use_global_device_ids=true, to_apply=%region_0.0 | all-reduce | flops 4096 | bytes 32768 | tf_op jit(solution)/shard_map/psum | solution.py:23
  145.9 0.9 fusion.6
  146.8 0.0 all-reduce.3.cloned.1.call-update
  146.8 0.0 reduce-scatter.2.cloned.1.call-start
  146.9 145.8 %all-reduce.3.cloned.1.call-done = f32[128,128]{0,1:T(8,128)} async-done(((f32[128,128]{0,1:T(8,128)}), f32[128,128]{0,1:T(8,128)}) %all-reduce.3.cloned.1.call-update) | async-done | bytes 65552 | tf_op jit(solution)/shard_map/psum | solution.py:24
  292.6 0.9 copy.8
  293.6 0.9 fusion.4
  294.4 11.7 %cholesky.16 = f32[128,128]{1,0:T(8,128)S(1)} custom-call(f32[128,128]{1,0:T(8,128)S(1)} %fusion.4), custom_call_target="Cholesky" | custom-call | tf_op jit(solution)/shard_map/jit(cholesky)/cholesky | solution.py:25
  306.2 0.6 compare_reduce_fusion
  306.8 0.7 fusion.2
  307.5 9.8 %custom-call.7 = f32[1,128,128]{1,2,0:T(8,128)S(1)} custom-call(f32[1,128,128]{2,1,0:T(8,128)S(1)} %fusion.2), custom_call_target="InvertDiagBlocksLowerTriangular" | custom-call | tf_op jit(solution)/shard_map/jit(_solve_triangular)/triangular_solve | solution.py:26
  317.3 0.2 convolution_convert_fusion
  317.5 2.7 fusion.14
  320.2 0.0 reduce-scatter.2.cloned.1.call-update
  320.2 0.0 all-reduce.5.cloned.1.call-start
  320.2 224.5 %reduce-scatter.2.cloned.1.call-done = f32[256,128]{1,0:T(8,128)} async-done(((f32[8192,128]{1,0:T(8,128)}), f32[256,128]{1,0:T(8,128)}) %reduce-scatter.2.cloned.1.call-update) | async-done | bytes 131088 | tf_op jit(solution)/shard_map/reduce_scatter | solution.py:29
  544.7 0.0 all-reduce.5.cloned.1.call-update
  544.7 0.0 all-gather.5.cloned.1.call-start
  544.8 119.4 %all-reduce.5.cloned.1.call-done = f32[256,128]{1,0:T(8,128)} async-done(((f32[256,128]{1,0:T(8,128)}), f32[256,128]{1,0:T(8,128)}) %all-reduce.5.cloned.1.call-update) | async-done | bytes 131088 | tf_op jit(solution)/shard_map/psum | solution.py:32
  664.2 1.6 fusion.12
  665.7 0.0 all-gather.5.cloned.1.call-update
  665.8 81.2 %all-gather.5.cloned.1.call-done = bf16[8192,128]{1,0:T(8,128)(2,1)} async-done(((bf16[256,128]{1,0:T(8,128)(2,1)}), bf16[8192,128]{1,0:T(8,128)(2,1)}) %all-gather.5.cloned.1.call-update) | async-done | bytes 2097168 | tf_op jit(solution)/shard_map/all_gather | solution.py:36
  747.0 0.0 copy-done
  747.0 0.0 copy-done.1
  747.0 0.0 copy-done.2
  747.0 3.6 subtract_bitcast_fusion
  (4 shorter events, 0.0 us)
Async XLA Ops:
  7.2 89.1 %all-gather.3.cloned.1.call-start = ((), (), s32[]{:S(2)}) async-start(), calls=%async_computation.1 | async-start | bytes 2162688 | tf_op jit(solution)/shard_map/all_gather | solution.py:20
  7.9 284.7 %all-reduce.3.cloned.1.call-start = ((), (), s32[]{:S(2)}) async-start(), calls=%async_computation.2 | async-start | bytes 131072 | tf_op jit(solution)/shard_map/psum | solution.py:24
  146.8 397.9 %reduce-scatter.2.cloned.1.call-start = ((), (), s32[]{:S(2)}) async-start(), calls=%async_computation.3 | async-start | bytes 4325376 | tf_op jit(solution)/shard_map/reduce_scatter | solution.py:29
  320.2 426.9 %copy-start = (f32[1,32,8192]{2,1,0:T(8,128)S(1)}, f32[1,32,8192]{2,1,0:T(8,128)}, u32[]{:S(2)}) copy-start(f32[1,32,8192]{2,1,0:T(8,128)} %param.6) | copy-start | bytes 3145732
  320.2 426.9 %copy-start.1 = (bf16[32,8192]{1,0:T(8,128)(2,1)S(1)}, bf16[32,8192]{1,0:T(8,128)(2,1)}, u32[]{:S(2)}) copy-start(bf16[32,8192]{1,0:T(8,128)(2,1)} %param.4) | copy-start | bytes 1572868
  320.2 426.9 %copy-start.2 = (bf16[1,32,8192]{2,1,0:T(8,128)(2,1)S(1)}, bf16[1,32,8192]{2,1,0:T(8,128)(2,1)}, u32[]{:S(2)}) copy-start(bf16[1,32,8192]{2,1,0:T(8,128)(2,1)} %param.5) | copy-start | bytes 1572868
  320.2 344.0 %all-reduce.5.cloned.1.call-start = ((), (), s32[]{:S(2)}) async-start(), calls=%async_computation.4 | async-start | bytes 262144 | tf_op jit(solution)/shard_map/psum | solution.py:32
  544.7 202.3 %all-gather.5.cloned.1.call-start = ((), (), s32[]{:S(2)}) async-start(), calls=%async_computation.5 | async-start | bytes 2162688 | tf_op jit(solution)/shard_map/all_gather | solution.py:36
Sparse Core Ops, SparseCore 0:
  11.2 85.0 all-gather.2
  146.9 145.6 all-reduce.2
  320.3 224.3 reduce-scatter.1
  547.0 117.1 all-reduce.4
  667.7 79.2 all-gather.4
where the time goes:
time: 760 us; the launch traced here: 757 us
  waiting for transfers between devices  658 us (87%)
  blocking collectives  47.6 us (6%)
  other arithmetic  27 us (4%)
  between operations  13.8 us (2%)
  matrix products  9.36 us (1%)
    reduce_scatter x1, waiting for transfers between devices, per_device(): lax.psum_scatter(column_product(columns, ortho_bf), 'fsdp', scatter_dimen...  224 us
    psum x1, waiting for transfers between devices, per_device(): lax.psum(jnp.dot(mean_p.T, mean_p, precision=lax.Precision.HIGHEST), 'fsdp')  146 us
    psum x1, waiting for transfers between devices, per_device(): new_q = lax.psum(shard, 'rep') / replicas  119 us
    all_gather x1, waiting for transfers between devices, per_device(): lax.all_gather(q_start, 'fsdp', axis=0, tiled=True)  86.6 us
    all_gather x1, waiting for transfers between devices, per_device(): lax.all_gather(q_bf, 'fsdp', axis=0, tiled=True)  81.2 us
    psum x1, blocking collectives, per_device(): mean_p = lax.psum(local_p, 'rep') / replicas  47.6 us
  transfers between devices with their start and end apart: 5, of which 5 were waited for; matrix products, arithmetic and copies ran while one was open for 0% of the time, Pallas kernels for 0%

commit v1 on v0

v1 whole, which is shorter than its diff:
```python
import jax
import jax.numpy as jnp
from jax import lax
from jax.experimental import pallas as pl
from jax.experimental.pallas import tpu as pltpu
from jax.sharding import PartitionSpec as P

HIGHEST = lax.Precision.HIGHEST
F32 = jnp.float32
BF16 = jnp.bfloat16
D, R, NREP, NF = 8192, 128, 16, 32
NX, NY, NZ = 4, 8, 8
ROWS = 32
COLS = D // NREP
QROWS = D // NF
VMEM = pl.BlockSpec(memory_space=pltpu.VMEM)
SMEM = pl.BlockSpec(memory_space=pltpu.SMEM)
LIGHT = pl.CostEstimate(flops=1, bytes_accessed=1, transcendentals=0)
WIDE = pltpu.CompilerParams(vmem_limit_bytes=60 * 1024 * 1024)
PARAMS = pltpu.CompilerParams(vmem_limit_bytes=32 * 1024 * 1024)


def dot(a, b, dims):
    return lax.dot_general(a, b, (dims, ((), ())), precision=HIGHEST, preferred_element_type=F32)


def transpose_groups(tiles):
    group = lax.broadcasted_iota(jnp.int32, tiles[0].shape, 1) // 16
    tiles = list(tiles)
    for step in (1, 2, 4):
        upper = (group & step) != 0
        for i in range(8):
            if i & step:
                continue
            x, y = tiles[i], tiles[i + step]
            tiles[i] = jnp.where(upper, pltpu.roll(y, 16 * step, 1), x)
            tiles[i + step] = jnp.where(upper, y, pltpu.roll(x, 128 - 16 * step, 1))
    return tiles


def tile_at(i, h):
    return slice(128 * (2 * i + h), 128 * (2 * i + h) + 128)


def share_kernel(place, q, out, sems):
    mine = q.at[pl.ds(pl.multiple_of(16 * place[0], 16), 16), :]
    copies = [pltpu.make_async_copy(mine, out.at[y], sems.at[y]) for y in range(NY)]
    for copy in copies:
        copy.start()
    for copy in copies:
        copy.wait()


def share(place, q):
    return pl.pallas_call(
        share_kernel,
        out_shape=jax.ShapeDtypeStruct((NY, 16, R), BF16),
        in_specs=[SMEM, pl.BlockSpec(memory_space=pltpu.HBM)],
        out_specs=VMEM,
        scratch_shapes=[pltpu.SemaphoreType.DMA((NY,))],
        compiler_params=WIDE,
        name="share",
    )(place, q)


def merge_kernel(parent, local, error, out, parent_v, local_v, error_v, sems):
    def copies(v):
        at = pl.ds(16 * v, 16)
        return [
            pltpu.make_async_copy(error.at[0, at, :], error_v.at[at, :], sems.at[2, v]),
            pltpu.make_async_copy(local.at[0, at, :], local_v.at[at, :], sems.at[1, v]),
            pltpu.make_async_copy(parent.at[at, :], parent_v.at[at, :], sems.at[0, v]),
        ]

    for v in range(2):
        for copy in copies(v):
            copy.start()
    for v in range(2):
        for copy in copies(v):
            copy.wait()
        rows = slice(16 * v, 16 * v + 16)
        for u in range(4):
            for h in range(2):
                tiles = []
                for i in range(8):
                    at = tile_at(8 * u + i, h)
                    merged = local_v[rows, at].astype(F32) - parent_v[rows, at].astype(F32) + error_v[rows, at]
                    tiles.append(merged.astype(BF16))
                for g, tile in enumerate(transpose_groups(tiles)):
                    out[2 * g + h, rows, 128 * u:128 * u + 128] = tile


def merge(parent, local, error):
    hbm = pl.BlockSpec(memory_space=pltpu.HBM)
    return pl.pallas_call(
        merge_kernel,
        out_shape=jax.ShapeDtypeStruct((NREP, ROWS, COLS), BF16),
        in_specs=[hbm, hbm, hbm],
        out_specs=VMEM,
        scratch_shapes=[pltpu.VMEM((ROWS, D), BF16), pltpu.VMEM((ROWS, D), BF16),
                        pltpu.VMEM((ROWS, D), F32), pltpu.SemaphoreType.DMA((3, 2))],
        compiler_params=WIDE,
        cost_estimate=LIGHT, name="merge",
    )(parent, local, error)


def left_kernel(got, q, s_out, p_out):
    s = got[0].astype(F32)
    for r in range(1, NREP):
        s = s + got[r].astype(F32)
    s_out[...] = s
    shares = [q[x, y] for y in range(NY) for x in range(NX)]
    p = dot(s, jnp.concatenate(shares, axis=0).astype(F32), ((1,), (0,)))
    for r in range(NREP):
        p_out[r] = p


def left(got, q):
    return pl.pallas_call(
        left_kernel,
        out_shape=(jax.ShapeDtypeStruct((ROWS, COLS), F32),
                   jax.ShapeDtypeStruct((NREP, ROWS, R), F32)),
        in_specs=[VMEM, VMEM], out_specs=(VMEM, VMEM), compiler_params=PARAMS, name="left",
    )(got, q)


def rows_kernel(parts, s, mean_out, z_out):
    p = parts[0]
    for r in range(1, NREP):
        p = p + parts[r]
    mean = p / NREP
    mean_out[...] = mean
    y = dot(s[...], mean, ((0,), (0,)))
    gram = dot(mean, mean, ((0,), (0,)))
    for f in range(NF):
        for b in range(4):
            z_out[f, :, 128 * b:128 * b + 128] = y[16 * f + 4 * b:16 * f + 4 * b + 4]
        z_out[f, :, COLS:] = gram[4 * f:4 * f + 4]


def rows(parts, s):
    return pl.pallas_call(
        rows_kernel,
        out_shape=(jax.ShapeDtypeStruct((ROWS, R), F32), jax.ShapeDtypeStruct((NF, 4, COLS + R), F32)),
        in_specs=[VMEM, VMEM], out_specs=(VMEM, VMEM), compiler_params=PARAMS, name="rows",
    )(parts, s)


def total_kernel(parts, out):
    t = parts[0]
    for i in range(1, parts.shape[0]):
        t = t + parts[i]
    for i in range(out.shape[0]):
        out[i] = t


def total(parts, copies):
    return pl.pallas_call(
        total_kernel,
        out_shape=jax.ShapeDtypeStruct((copies,) + parts.shape[1:], F32),
        in_specs=[VMEM], out_specs=VMEM, compiler_params=PARAMS, name="total",
    )(parts)


def square(p, x):
    wide = jnp.concatenate([p, x], axis=1)
    high = wide.astype(BF16).astype(F32)
    rest = wide - high
    mid = rest.astype(BF16).astype(F32)
    low = rest - mid
    a = jnp.concatenate([high, high, mid, high, low, mid], axis=0)[:, :R].astype(BF16)
    b = jnp.concatenate([high, mid, high, low, high, mid], axis=0).astype(BF16)
    return lax.dot_general(a, b, (((0,), (0,)), ((), ())), preferred_element_type=F32)


def inverse_factor(gram):
    def spread(x):
        return jnp.broadcast_to(x, (8, R))

    row = lax.broadcasted_iota(jnp.int32, (R, R), 0)
    col = lax.broadcasted_iota(jnp.int32, (R, R), 1)
    unit = (row == col).astype(F32)
    sub = lax.broadcasted_iota(jnp.int32, (8, R), 0)
    count = R // 8
    left = [gram[8 * g:8 * g + 8] for g in range(count)]
    right = [unit[8 * g:8 * g + 8] for g in range(count)]
    for k in range(count):
        last = k == count - 1
        p, x = left[k], right[k]
        d = [spread(p[:, 8 * k + j:8 * k + j + 1]) for j in range(8)]
        if not last:
            n, y = left[k + 1], right[k + 1]
            c = [spread(n[:, 8 * k + j:8 * k + j + 1]) for j in range(8)]
        e = {(i, j): spread(d[j][i:i + 1]) for j in range(8) for i in range(j, 8)}
        for j in range(8):
            inv = lax.rsqrt(e[j, j])
            low = {i: e[i, j] * inv for i in range(j + 1, 8)}
            for m in range(j + 1, 8):
                for i in range(m, 8):
                    e[i, m] = e[i, m] - low[i] * low[m]
            p_row, x_row = spread(p[j:j + 1]) * inv, spread(x[j:j + 1]) * inv
            if j < 7:
                here = jnp.where(sub > j, d[j] * inv, 0.0)
                for m in range(j + 1, 8):
                    d[m] = d[m] - here * low[m]
                p, x = p - here * p_row, x - here * x_row
            p, x = jnp.where(sub == j, p_row, p), jnp.where(sub == j, x_row, x)
            if not last:
                below = c[j] * inv
                for m in range(j + 1, 8):
                    c[m] = c[m] - below * low[m]
                n, y = n - below * p_row, y - below * x_row
        right[k] = x
        if not last:
            left[k + 1], right[k + 1] = n, y
        if k < count - 2:
            update = square(p, x)
            for g in range(k + 2, count):
                left[g] = left[g] - update[8 * g:8 * g + 8, :R]
                right[g] = right[g] - update[8 * g:8 * g + 8, R:]
    return jnp.concatenate(right, axis=0)


def solve_kernel(shard, sums, mean, out, gram, y, q_all):
    for f in range(NF):
        gram[4 * f:4 * f + 4, :] = sums[f, :, COLS:]
        for b in range(4):
            y[16 * f + 4 * b:16 * f + 4 * b + 4, :] = sums[f, :, 128 * b:128 * b + 128]
    linv = inverse_factor(gram[...])
    ortho = dot(mean[...], linv, ((1,), (1,))).astype(BF16)
    q = dot(y[...], linv, ((1,), (1,))) / NREP
    q_all[...] = q
    approx = lax.dot_general(
        ortho, q.astype(BF16), (((1,), (1,)), ((), ())), preferred_element_type=F32).astype(BF16)
    own = q_all[pl.ds(pl.multiple_of(16 * shard[0], 16), 16), :]
    high = own.astype(BF16)
    low = (own - high.astype(F32)).astype(BF16)
    for z in range(NZ):
        out[z, :, :COLS] = approx
        out[z, :16, COLS:] = high
        out[z, 16:, COLS:] = low


def solve(shard, sums, mean):
    return pl.pallas_call(
        solve_kernel,
        out_shape=jax.ShapeDtypeStruct((NZ, ROWS, COLS + R), BF16),
        in_specs=[SMEM, VMEM, VMEM],
        out_specs=VMEM,
        scratch_shapes=[pltpu.VMEM((R, R), F32), pltpu.VMEM((COLS, R), F32), pltpu.VMEM((COLS, R), F32)],
        compiler_params=PARAMS,
        name="solve",
    )(shard, sums, mean)


def finish_kernel(core, parent, local, error, mine, other, update, new_error, new_q,
                  update_v, error_v, q_v, sems):
    copies = []

    def send(source, target):
        copies.append(pltpu.make_async_copy(source, target, sems.at[len(copies)]))
        copies[-1].start()

    parts = (mine, core[0]), (other, 1 - core[0])
    for got, sender in parts:
        for z in range(NZ):
            part = got[z, :, COLS:].astype(F32)
            at = pl.ds(pl.multiple_of(16 * z + QROWS // 2 * sender, 16), 16)
            q_v[at, :] = part[:16] + part[16:]
    send(q_v, new_q)
    for u in range(4):
        for got, sender in parts:
            tiles = transpose_groups([got[z, :, 128 * u:128 * u + 128] for z in range(NZ)])
            for i, approx in enumerate(tiles):
                at = pl.ds(pl.multiple_of(256 * (8 * u + i) + 128 * sender, 128), 128)
                merged = local[0, :, at].astype(F32) - parent[:, at].astype(F32) + error[0, :, at]
                update_v[:, at] = approx
                error_v[:, at] = merged - approx.astype(F32)
        at = pl.ds(u * (D // 4), D // 4)
        send(update_v.at[:, at], update.at[:, at])
        send(error_v.at[:, at], new_error.at[0, :, at])
    for copy in copies:
        copy.wait()


def finish(core, parent, local, error, mine, other):
    hbm = pl.BlockSpec(memory_space=pltpu.HBM)
    return pl.pallas_call(
        finish_kernel,
        out_shape=(jax.ShapeDtypeStruct((ROWS, D), BF16), jax.ShapeDtypeStruct((1, ROWS, D), F32),
                   jax.ShapeDtypeStruct((QROWS, R), F32)),
        in_specs=[SMEM, VMEM, VMEM, VMEM, VMEM, VMEM],
        out_specs=(hbm, hbm, hbm),
        scratch_shapes=[pltpu.VMEM((ROWS, D), BF16), pltpu.VMEM((ROWS, D), F32),
                        pltpu.VMEM((QROWS, R), F32), pltpu.SemaphoreType.DMA((9,))],
        compiler_params=PARAMS,
        name="finish",
    )(core, parent, local, error, mine, other)


def exchange(x, axis):
    return lax.all_to_all(x, axis, 0, 0, tiled=True)


def swap(x):
    return lax.ppermute(x, "core", [(0, 1), (1, 0)])


def per_device(parent, local_weights, error, q_start):
    rep, fsdp = ("z", "core"), ("y", "x")
    core, f = (lax.axis_index(axis) for axis in ("core", fsdp))
    r = lax.axis_index(("core", "z"))
    q = exchange(share(r[None], q_start), "y")
    merged, q = lax.optimization_barrier((merge(parent, local_weights, error), q))
    q = lax.all_gather(q, "x")
    s, p = left(exchange(merged, rep), q)
    mean, z = rows(exchange(p, rep), s)
    z = exchange(total(exchange(z, fsdp), NF), fsdp)
    got = exchange(solve(f[None], z, mean), "z")
    return finish(core[None], parent, local_weights, error, got, swap(got))


def solution(mesh):
    mesh = jax.sharding.Mesh(mesh.devices.reshape(8, 2, 8, 4), ("z", "core", "y", "x"))
    rep, fsdp = ("z", "core"), ("y", "x")
    placed = (P(fsdp, None), P(rep, fsdp, None), P(rep, fsdp, None), P(fsdp, None))
    return jax.shard_map(
        per_device,
        mesh=mesh,
        in_specs=placed,
        out_specs=(P(fsdp, None), P(rep, fsdp, None), P(fsdp, None)),
        check_vma=False,
    )
```

time: 760 us -> 124 us (0.16)
  waiting for transfers between devices: 658 us -> 24.5 us
  starting transfers between devices: 0.2 us -> 30.2 us
  other arithmetic: 27 us -> 0 us
  between operations: 13.8 us -> 0.71 us
  Pallas kernels: 0 us -> 12.6 us
  matrix products: 9.36 us -> 0 us
  blocking collectives: 47.6 us -> 55.4 us
    psum x2 -> x0, waiting for transfers between devices: 265 us -> none  [the longest x1 146 us: per_device(): lax.psum(jnp.dot(mean_p.T, mean_p, precision=lax.Precision.HIGHEST), 'fsdp')]
    reduce_scatter x1 -> x0, waiting for transfers between devices: 224 us -> none  [per_device(): lax.psum_scatter(column_product(columns, ortho_bf), 'fsdp', scatter_dimen...]
    all_gather x2 -> x0, waiting for transfers between devices: 168 us -> none  [the longest x1 86.6 us: per_device(): lax.all_gather(q_start, 'fsdp', axis=0, tiled=True)]
    psum x1 -> x0, blocking collectives: 47.6 us -> none  [per_device(): mean_p = lax.psum(local_p, 'rep') / replicas]
    all_to_all x0 -> x3, blocking collectives: none -> 45.1 us  [exchange(): return lax.all_to_all(x, axis, 0, 0, tiled=True)]
    all_to_all x0 -> x3, starting transfers between devices: none -> 24 us  [exchange(): return lax.all_to_all(x, axis, 0, 0, tiled=True)]
    all_to_all x0 -> x3, waiting for transfers between devices: none -> 23.2 us  [exchange(): return lax.all_to_all(x, axis, 0, 0, tiled=True)]
    another operation x5 -> x0, other arithmetic: 22.9 us -> none  [the longest x3 12.4 us: per_device(): lower = jnp.linalg.cholesky(gram)]
  transfers between devices with their start and end apart: 5 -> 4, of which waited for: 5 -> 4; matrix products, arithmetic and copies ran while one was open for 0% -> 0% of each run, Pallas kernels for 0% -> 2%
where the time goes in v1:
time: 124 us; the launch traced here: 123 us
  blocking collectives  55.4 us (45%)
  starting transfers between devices  30.2 us (24%)
  waiting for transfers between devices  24.5 us (20%)
  Pallas kernels  12.6 us (10%)
    all_to_all x3, blocking collectives, exchange(): return lax.all_to_all(x, axis, 0, 0, tiled=True)  45.1 us
    all_to_all x3, starting transfers between devices, exchange(): return lax.all_to_all(x, axis, 0, 0, tiled=True)  24 us
    all_to_all x3, waiting for transfers between devices, exchange(): return lax.all_to_all(x, axis, 0, 0, tiled=True)  23.2 us
    all_gather x1, blocking collectives, per_device(): q = lax.all_gather(q, 'x')  10.4 us
    ppermute x1, starting transfers between devices, swap(): return lax.ppermute(x, 'core', [(0, 1), (1, 0)])  6.21 us
    pallas_call x1, Pallas kernels, solve(): pl.pallas_call(solve_kernel, out_shape=jax.ShapeDtypeStruct((NZ, ROWS, CO...  4.54 us
    pallas_call x1, Pallas kernels, merge(): pl.pallas_call(merge_kernel, out_shape=jax.ShapeDtypeStruct((NREP, ROWS,...  2.78 us
  transfers between devices with their start and end apart: 4, of which 4 were waited for; matrix products, arithmetic and copies ran while one was open for 0% of the time, Pallas kernels for 2%

profile of v1, /device:TPU:1, one launch (start us, length us, event | category | flops | bytes accessed | tf_op | source)
XLA Modules:
  0.0 123.4 jit_solution(1314853938976150579)
XLA Ops:
  0.6 1.7 %share.1 = bf16[8,16,128]{2,1,0:T(8,128)(2,1)} custom-call(s32[1]{0:T(128)} %bitcast.2.place, bf16[256,128]{1,0:T(8,128)(2,1)} %q.1), custom_call_target="tpu_custom_call" | custom-call | tf_op jit(solution)/shard_map/share/pallas_call | solution.py:55
  2.3 7.7 %all-to-all-start = ((bf16[8,16,128]{2,1,0:T(8,128)(2,1)}), bf16[8,16,128]{2,1,0:T(8,128)(2,1)S(1)}, u32[]{:S(2)}, u32[]{:S(2)}) async-start(bf16[8,16,128]{2,1,0:T(8,128)(2,1)} %share.1), calls=%async_computation | async-start | bytes 65536 | tf_op jit(solution)/shard_map/all_to_all | solution.py:302
  10.0 2.8 %merge.1 = bf16[16,32,512]{2,1,0:T(8,128)(2,1)} custom-call(bf16[32,8192]{1,0:T(8,128)(2,1)} %parent.3, bf16[1,32,8192]{2,1,0:T(8,128)(2,1)} %local.3, f32[1,32,8192]{2,1,0:T(8,128)} %error.3), custom_call_target="tpu_custom_call" | custom-call | flops 1 | bytes 1 | tf_op jit(solution)/shard_map/merge/pallas_call | solution.py:95
  12.8 4.2 %all-to-all-done = bf16[8,16,128]{2,1,0:T(8,128)(2,1)S(1)} async-done(((bf16[8,16,128]{2,1,0:T(8,128)(2,1)}), bf16[8,16,128]{2,1,0:T(8,128)(2,1)S(1)}, u32[]{:S(2)}, u32[]{:S(2)}) %all-to-all-start) | async-done | bytes 32800 | tf_op jit(solution)/shard_map/all_to_all | solution.py:302
  16.9 12.3 %all-to-all-start.1 = ((bf16[16,32,512]{2,1,0:T(8,128)(2,1)}), bf16[16,32,512]{2,1,0:T(8,128)(2,1)S(1)}, u32[]{:S(2)}, u32[]{:S(2)}) async-start(bf16[16,32,512]{2,1,0:T(8,128)(2,1)} %merge.1), calls=%async_computation.1 | async-start | bytes 1048576 | tf_op jit(solution)/shard_map/all_to_all | solution.py:302
  29.3 10.4 %all-gather = bf16[32,16,128]{2,1,0:T(8,128)(2,1)S(1)} all-gather(bf16[8,16,128]{2,1,0:T(8,128)(2,1)S(1)} %all-to-all-done), channel_id=2, replica_groups=mesh['z'=8,'core'=2,'y'=8,'x'=4] {'x'}, dimensions={0}, use_global_device_ids=true | all-gather | bytes 163840 | tf_op jit(solution)/shard_map/all_gather | solution.py:315
  39.6 7.0 %all-to-all-done.1.got = bf16[16,32,512]{2,1,0:T(8,128)(2,1)S(1)} async-done(((bf16[16,32,512]{2,1,0:T(8,128)(2,1)}), bf16[16,32,512]{2,1,0:T(8,128)(2,1)S(1)}, u32[]{:S(2)}, u32[]{:S(2)}) %all-to-all-start.1) | async-done | bytes 524320 | tf_op jit(solution)/shard_map/all_to_all | solution.py:302
  46.6 0.3 left.1
  46.9 14.4 %all_to_all.30.parts = f32[16,32,128]{2,1,0:T(8,128)S(1)} all-to-all(f32[16,32,128]{2,1,0:T(8,128)S(1)} %get-tuple-element.11), channel_id=1, replica_groups=mesh['z'=8,'core'=2,'y'=8,'x'=4] {'z','core'}, dimensions={0} | all-to-all | bytes 524288 | tf_op jit(solution)/shard_map/all_to_all | solution.py:302
  61.3 0.5 rows.1
  61.8 18.4 %all_to_all.31.parts = f32[32,4,640]{2,1,0:T(4,128)S(1)} all-to-all(f32[32,4,640]{2,1,0:T(4,128)S(1)} %get-tuple-element.13), channel_id=1, replica_groups=mesh['z'=8,'core'=2,'y'=8,'x'=4] {'y','x'}, dimensions={0} | all-to-all | bytes 655360 | tf_op jit(solution)/shard_map/all_to_all | solution.py:302
  80.2 0.0 copy-start.2
  80.2 0.8 total.1
  80.9 0.0 copy-start
  80.9 4.0 %all-to-all-start.4 = ((f32[32,4,640]{2,1,0:T(4,128)}), f32[32,4,640]{2,1,0:T(4,128)S(1)}, u32[]{:S(2)}, u32[]{:S(2)}) async-start(f32[32,4,640]{2,1,0:T(4,128)} %total.1), calls=%async_computation.4 | async-start | bytes 655360 | tf_op jit(solution)/shard_map/all_to_all | solution.py:302
  85.0 12.1 %all-to-all-done.4.sums = f32[32,4,640]{2,1,0:T(4,128)S(1)} async-done(((f32[32,4,640]{2,1,0:T(4,128)}), f32[32,4,640]{2,1,0:T(4,128)S(1)}, u32[]{:S(2)}, u32[]{:S(2)}) %all-to-all-start.4) | async-done | bytes 327712 | tf_op jit(solution)/shard_map/all_to_all | solution.py:302
  97.1 0.0 copy-start.1
  97.1 4.5 %solve.1 = bf16[8,32,640]{2,1,0:T(8,128)(2,1)S(1)} custom-call(s32[1]{0:T(128)} %bitcast.1.shard, f32[32,4,640]{2,1,0:T(4,128)S(1)} %all-to-all-done.4.sums, f32[32,128]{1,0:T(8,128)S(1)} %get-tuple-element.14.mean), custom_call_target="tpu_custom_call" | custom-call | tf_op jit(solution)/shard_map/solve/pallas_call | solution.py:245
  101.6 12.3 %all_to_all.32.mine = bf16[8,32,640]{2,1,0:T(8,128)(2,1)S(1)} all-to-all(bf16[8,32,640]{2,1,0:T(8,128)(2,1)S(1)} %solve.1), channel_id=1, replica_groups=mesh['z'=8,'core'=2,'y'=8,'x'=4] {'z'}, dimensions={0} | all-to-all | bytes 655360 | tf_op jit(solution)/shard_map/all_to_all | solution.py:302
  113.9 6.2 %collective-permute-start = (bf16[8,32,640]{2,1,0:T(8,128)(2,1)S(1)}, bf16[8,32,640]{2,1,0:T(8,128)(2,1)S(1)}, u32[]{:S(2)}, u32[]{:S(2)}) collective-permute-start(bf16[8,32,640]{2,1,0:T(8,128)(2,1)S(1)} %all_to_all.32.mine), channel_id=1, source_target_pairs={{0,32},{32,0},{1,33},{33,1},{2,34},{34,2},{3,35},{35,3},{4,36},{36... | collective-permute-start | bytes 983048 | tf_op jit(solution)/shard_map/ppermute | solution.py:306
  120.1 1.2 collective-permute-done.other
  121.4 0.0 copy-done.2
  121.4 0.0 copy-done
  121.4 0.0 copy-done.1
  121.4 2.1 %finish.1 = (bf16[32,8192]{1,0:T(8,128)(2,1)}, f32[1,32,8192]{2,1,0:T(8,128)}, f32[256,128]{1,0:T(8,128)}) custom-call(s32[1]{0:T(128)} %bitcast.core, bf16[32,8192]{1,0:T(8,128)(2,1)S(1)} %copy-done.1, bf16[1,32,8192]{2,1,0:T(8,128)(2,1)S(1)} %copy-done.2, f32[1,32,8192]{2,1,0:T(8,128)S(1)} %copy-done, bf16[8,32,640]{2,1,0:T(8,128)(2,1)S(1)} %all_to_all.32.mine, ...), custom_call_target="tpu_custom_call" | custom-call | tf_op jit(solution)/shard_map/finish/pallas_call | solution.py:288
Async XLA Ops:
  2.3 14.6 %all-to-all-start = ((bf16[8,16,128]{2,1,0:T(8,128)(2,1)}), bf16[8,16,128]{2,1,0:T(8,128)(2,1)S(1)}, u32[]{:S(2)}, u32[]{:S(2)}) async-start(bf16[8,16,128]{2,1,0:T(8,128)(2,1)} %share.1), calls=%async_computation | async-start | bytes 65536 | tf_op jit(solution)/shard_map/all_to_all | solution.py:302
  16.9 29.7 %all-to-all-start.1 = ((bf16[16,32,512]{2,1,0:T(8,128)(2,1)}), bf16[16,32,512]{2,1,0:T(8,128)(2,1)S(1)}, u32[]{:S(2)}, u32[]{:S(2)}) async-start(bf16[16,32,512]{2,1,0:T(8,128)(2,1)} %merge.1), calls=%async_computation.1 | async-start | bytes 1048576 | tf_op jit(solution)/shard_map/all_to_all | solution.py:302
  80.2 41.2 %copy-start.2 = (bf16[1,32,8192]{2,1,0:T(8,128)(2,1)S(1)}, bf16[1,32,8192]{2,1,0:T(8,128)(2,1)}, u32[]{:S(2)}) copy-start(bf16[1,32,8192]{2,1,0:T(8,128)(2,1)} %local.3) | copy-start | bytes 1572868
  80.9 40.4 %copy-start = (f32[1,32,8192]{2,1,0:T(8,128)S(1)}, f32[1,32,8192]{2,1,0:T(8,128)}, u32[]{:S(2)}) copy-start(f32[1,32,8192]{2,1,0:T(8,128)} %error.3) | copy-start | bytes 3145732
  80.9 16.1 %all-to-all-start.4 = ((f32[32,4,640]{2,1,0:T(4,128)}), f32[32,4,640]{2,1,0:T(4,128)S(1)}, u32[]{:S(2)}, u32[]{:S(2)}) async-start(f32[32,4,640]{2,1,0:T(4,128)} %total.1), calls=%async_computation.4 | async-start | bytes 655360 | tf_op jit(solution)/shard_map/all_to_all | solution.py:302
  97.1 24.3 %copy-start.1 = (bf16[32,8192]{1,0:T(8,128)(2,1)S(1)}, bf16[32,8192]{1,0:T(8,128)(2,1)}, u32[]{:S(2)}) copy-start(bf16[32,8192]{1,0:T(8,128)(2,1)} %parent.3) | copy-start | bytes 1572868
  113.9 7.4 %collective-permute-start = (bf16[8,32,640]{2,1,0:T(8,128)(2,1)S(1)}, bf16[8,32,640]{2,1,0:T(8,128)(2,1)S(1)}, u32[]{:S(2)}, u32[]{:S(2)}) collective-permute-start(bf16[8,32,640]{2,1,0:T(8,128)(2,1)S(1)} %all_to_all.32.mine), channel_id=1, source_target_pairs={{0,32},{32,0},{1,33},{33,1},{2,34},{34,2},{3,35},{35,3},{4,36},{36... | collective-permute-start | bytes 983048 | tf_op jit(solution)/shard_map/ppermute | solution.py:306

commit v2 on v1

--- a/solution.py
+++ b/solution.py
@@ -40,6 +40,19 @@
 
 def tile_at(i, h):
     return slice(128 * (2 * i + h), 128 * (2 * i + h) + 128)
+
+
+def thirds(x):
+    high = x.astype(BF16).astype(F32)
+    mid = (x - high).astype(BF16).astype(F32)
+    return high, mid, x - high - mid
+
+
+def cross(a, b):
+    (ah, am, al), (bh, bm, bl) = thirds(a), thirds(b)
+    a = jnp.concatenate([ah, ah, am, ah, al, am], axis=0).astype(BF16)
+    b = jnp.concatenate([bh, bm, bh, bl, bh, bm], axis=0).astype(BF16)
+    return lax.dot_general(a, b, (((0,), (0,)), ((), ())), preferred_element_type=F32)
 
 
 def share_kernel(place, q, out, sems):
@@ -110,7 +123,8 @@
         s = s + got[r].astype(F32)
     s_out[...] = s
     shares = [q[x, y] for y in range(NY) for x in range(NX)]
-    p = dot(s, jnp.concatenate(shares, axis=0).astype(F32), ((1,), (0,)))
+    q_all = jnp.concatenate(shares, axis=0)
+    p = sum(jnp.dot(part.astype(BF16), q_all, preferred_element_type=F32) for part in thirds(s))
     for r in range(NREP):
         p_out[r] = p
 
@@ -130,8 +144,8 @@
         p = p + parts[r]
     mean = p / NREP
     mean_out[...] = mean
-    y = dot(s[...], mean, ((0,), (0,)))
-    gram = dot(mean, mean, ((0,), (0,)))
+    y = cross(s[...], mean)
+    gram = cross(mean, mean)
     for f in range(NF):
         for b in range(4):
             z_out[f, :, 128 * b:128 * b + 128] = y[16 * f + 4 * b:16 * f + 4 * b + 4]
@@ -160,17 +174,6 @@
         out_shape=jax.ShapeDtypeStruct((copies,) + parts.shape[1:], F32),
         in_specs=[VMEM], out_specs=VMEM, compiler_params=PARAMS, name="total",
     )(parts)
-
-
-def square(p, x):
-    wide = jnp.concatenate([p, x], axis=1)
-    high = wide.astype(BF16).astype(F32)
-    rest = wide - high
-    mid = rest.astype(BF16).astype(F32)
-    low = rest - mid
-    a = jnp.concatenate([high, high, mid, high, low, mid], axis=0)[:, :R].astype(BF16)
-    b = jnp.concatenate([high, mid, high, low, high, mid], axis=0).astype(BF16)
-    return lax.dot_general(a, b, (((0,), (0,)), ((), ())), preferred_element_type=F32)
 
 
 def inverse_factor(gram):
@@ -214,7 +217,7 @@
         if not last:
             left[k + 1], right[k + 1] = n, y
         if k < count - 2:
-            update = square(p, x)
+            update = cross(p, jnp.concatenate([p, x], axis=1))
             for g in range(k + 2, count):
                 left[g] = left[g] - update[8 * g:8 * g + 8, :R]
                 right[g] = right[g] - update[8 * g:8 * g + 8, R:]

time: 124 us -> 124 us (level)
  no operation moved by 1% of the time
where the time goes in v2:
time: 124 us; the launch traced here: 123 us
  blocking collectives  55.4 us (45%)
  starting transfers between devices  30.2 us (24%)
  waiting for transfers between devices  24.5 us (20%)
  Pallas kernels  12.4 us (10%)
    all_to_all x3, blocking collectives, exchange(): return lax.all_to_all(x, axis, 0, 0, tiled=True)  45.1 us
    all_to_all x3, starting transfers between devices, exchange(): return lax.all_to_all(x, axis, 0, 0, tiled=True)  24 us
    all_to_all x3, waiting for transfers between devices, exchange(): return lax.all_to_all(x, axis, 0, 0, tiled=True)  23.2 us
    all_gather x1, blocking collectives, per_device(): q = lax.all_gather(q, 'x')  10.4 us
    ppermute x1, starting transfers between devices, swap(): return lax.ppermute(x, 'core', [(0, 1), (1, 0)])  6.21 us
    pallas_call x1, Pallas kernels, solve(): pl.pallas_call(solve_kernel, out_shape=jax.ShapeDtypeStruct((NZ, ROWS, CO...  4.54 us
    pallas_call x1, Pallas kernels, merge(): pl.pallas_call(merge_kernel, out_shape=jax.ShapeDtypeStruct((NREP, ROWS,...  2.78 us
  transfers between devices with their start and end apart: 4, of which 4 were waited for; matrix products, arithmetic and copies ran while one was open for 0% of the time, Pallas kernels for 2%

profile of v2, /device:TPU:1, one launch (start us, length us, event | category | flops | bytes accessed | tf_op | source)
XLA Modules:
  0.0 123.2 jit_solution(8807789531096731072)
XLA Ops:
  0.6 1.7 %share.1 = bf16[8,16,128]{2,1,0:T(8,128)(2,1)} custom-call(s32[1]{0:T(128)} %bitcast.2.place, bf16[256,128]{1,0:T(8,128)(2,1)} %q.1), custom_call_target="tpu_custom_call" | custom-call | tf_op jit(solution)/shard_map/share/pallas_call | solution.py:68
  2.3 7.7 %all-to-all-start = ((bf16[8,16,128]{2,1,0:T(8,128)(2,1)}), bf16[8,16,128]{2,1,0:T(8,128)(2,1)S(1)}, u32[]{:S(2)}, u32[]{:S(2)}) async-start(bf16[8,16,128]{2,1,0:T(8,128)(2,1)} %share.1), calls=%async_computation | async-start | bytes 65536 | tf_op jit(solution)/shard_map/all_to_all | solution.py:305
  10.0 2.8 %merge.1 = bf16[16,32,512]{2,1,0:T(8,128)(2,1)} custom-call(bf16[32,8192]{1,0:T(8,128)(2,1)} %parent.3, bf16[1,32,8192]{2,1,0:T(8,128)(2,1)} %local.3, f32[1,32,8192]{2,1,0:T(8,128)} %error.3), custom_call_target="tpu_custom_call" | custom-call | flops 1 | bytes 1 | tf_op jit(solution)/shard_map/merge/pallas_call | solution.py:108
  12.8 4.2 %all-to-all-done = bf16[8,16,128]{2,1,0:T(8,128)(2,1)S(1)} async-done(((bf16[8,16,128]{2,1,0:T(8,128)(2,1)}), bf16[8,16,128]{2,1,0:T(8,128)(2,1)S(1)}, u32[]{:S(2)}, u32[]{:S(2)}) %all-to-all-start) | async-done | bytes 32800 | tf_op jit(solution)/shard_map/all_to_all | solution.py:305
  16.9 12.3 %all-to-all-start.1 = ((bf16[16,32,512]{2,1,0:T(8,128)(2,1)}), bf16[16,32,512]{2,1,0:T(8,128)(2,1)S(1)}, u32[]{:S(2)}, u32[]{:S(2)}) async-start(bf16[16,32,512]{2,1,0:T(8,128)(2,1)} %merge.1), calls=%async_computation.1 | async-start | bytes 1048576 | tf_op jit(solution)/shard_map/all_to_all | solution.py:305
  29.3 10.4 %all-gather = bf16[32,16,128]{2,1,0:T(8,128)(2,1)S(1)} all-gather(bf16[8,16,128]{2,1,0:T(8,128)(2,1)S(1)} %all-to-all-done), channel_id=2, replica_groups=mesh['z'=8,'core'=2,'y'=8,'x'=4] {'x'}, dimensions={0}, use_global_device_ids=true | all-gather | bytes 163840 | tf_op jit(solution)/shard_map/all_gather | solution.py:318
  39.6 7.0 %all-to-all-done.1.got = bf16[16,32,512]{2,1,0:T(8,128)(2,1)S(1)} async-done(((bf16[16,32,512]{2,1,0:T(8,128)(2,1)}), bf16[16,32,512]{2,1,0:T(8,128)(2,1)S(1)}, u32[]{:S(2)}, u32[]{:S(2)}) %all-to-all-start.1) | async-done | bytes 524320 | tf_op jit(solution)/shard_map/all_to_all | solution.py:305
  46.6 0.3 left.1
  46.9 14.4 %all_to_all.30.parts = f32[16,32,128]{2,1,0:T(8,128)S(1)} all-to-all(f32[16,32,128]{2,1,0:T(8,128)S(1)} %get-tuple-element.11), channel_id=1, replica_groups=mesh['z'=8,'core'=2,'y'=8,'x'=4] {'z','core'}, dimensions={0} | all-to-all | bytes 524288 | tf_op jit(solution)/shard_map/all_to_all | solution.py:305
  61.3 0.3 rows.1
  61.6 18.4 %all_to_all.31.parts = f32[32,4,640]{2,1,0:T(4,128)S(1)} all-to-all(f32[32,4,640]{2,1,0:T(4,128)S(1)} %get-tuple-element.13), channel_id=1, replica_groups=mesh['z'=8,'core'=2,'y'=8,'x'=4] {'y','x'}, dimensions={0} | all-to-all | bytes 655360 | tf_op jit(solution)/shard_map/all_to_all | solution.py:305
  80.0 0.0 copy-start.2
  80.0 0.8 total.1
  80.7 0.0 copy-start
  80.7 4.0 %all-to-all-start.4 = ((f32[32,4,640]{2,1,0:T(4,128)}), f32[32,4,640]{2,1,0:T(4,128)S(1)}, u32[]{:S(2)}, u32[]{:S(2)}) async-start(f32[32,4,640]{2,1,0:T(4,128)} %total.1), calls=%async_computation.4 | async-start | bytes 655360 | tf_op jit(solution)/shard_map/all_to_all | solution.py:305
  84.8 12.1 %all-to-all-done.4.sums = f32[32,4,640]{2,1,0:T(4,128)S(1)} async-done(((f32[32,4,640]{2,1,0:T(4,128)}), f32[32,4,640]{2,1,0:T(4,128)S(1)}, u32[]{:S(2)}, u32[]{:S(2)}) %all-to-all-start.4) | async-done | bytes 327712 | tf_op jit(solution)/shard_map/all_to_all | solution.py:305
  96.9 0.0 copy-start.1
  96.9 4.5 %solve.1 = bf16[8,32,640]{2,1,0:T(8,128)(2,1)S(1)} custom-call(s32[1]{0:T(128)} %bitcast.1.shard, f32[32,4,640]{2,1,0:T(4,128)S(1)} %all-to-all-done.4.sums, f32[32,128]{1,0:T(8,128)S(1)} %get-tuple-element.14.mean), custom_call_target="tpu_custom_call" | custom-call | tf_op jit(solution)/shard_map/solve/pallas_call | solution.py:248
  101.4 12.3 %all_to_all.32.mine = bf16[8,32,640]{2,1,0:T(8,128)(2,1)S(1)} all-to-all(bf16[8,32,640]{2,1,0:T(8,128)(2,1)S(1)} %solve.1), channel_id=1, replica_groups=mesh['z'=8,'core'=2,'y'=8,'x'=4] {'z'}, dimensions={0} | all-to-all | bytes 655360 | tf_op jit(solution)/shard_map/all_to_all | solution.py:305
  113.7 6.2 %collective-permute-start = (bf16[8,32,640]{2,1,0:T(8,128)(2,1)S(1)}, bf16[8,32,640]{2,1,0:T(8,128)(2,1)S(1)}, u32[]{:S(2)}, u32[]{:S(2)}) collective-permute-start(bf16[8,32,640]{2,1,0:T(8,128)(2,1)S(1)} %all_to_all.32.mine), channel_id=1, source_target_pairs={{0,32},{32,0},{1,33},{33,1},{2,34},{34,2},{3,35},{35,3},{4,36},{36... | collective-permute-start | bytes 983048 | tf_op jit(solution)/shard_map/ppermute | solution.py:309
  119.9 1.2 %collective-permute-done.other = bf16[8,32,640]{2,1,0:T(8,128)(2,1)S(1)} collective-permute-done((bf16[8,32,640]{2,1,0:T(8,128)(2,1)S(1)}, bf16[8,32,640]{2,1,0:T(8,128)(2,1)S(1)}, u32[]{:S(2)}, u32[]{:S(2)}) %collective-permute-start) | collective-permute-done | bytes 327712 | tf_op jit(solution)/shard_map/ppermute | solution.py:309
  121.2 0.0 copy-done.2
  121.2 0.0 copy-done
  121.2 0.0 copy-done.1
  121.2 2.1 %finish.1 = (bf16[32,8192]{1,0:T(8,128)(2,1)}, f32[1,32,8192]{2,1,0:T(8,128)}, f32[256,128]{1,0:T(8,128)}) custom-call(s32[1]{0:T(128)} %bitcast.core, bf16[32,8192]{1,0:T(8,128)(2,1)S(1)} %copy-done.1, bf16[1,32,8192]{2,1,0:T(8,128)(2,1)S(1)} %copy-done.2, f32[1,32,8192]{2,1,0:T(8,128)S(1)} %copy-done, bf16[8,32,640]{2,1,0:T(8,128)(2,1)S(1)} %all_to_all.32.mine, ...), custom_call_target="tpu_custom_call" | custom-call | tf_op jit(solution)/shard_map/finish/pallas_call | solution.py:291
Async XLA Ops:
  2.3 14.6 %all-to-all-start = ((bf16[8,16,128]{2,1,0:T(8,128)(2,1)}), bf16[8,16,128]{2,1,0:T(8,128)(2,1)S(1)}, u32[]{:S(2)}, u32[]{:S(2)}) async-start(bf16[8,16,128]{2,1,0:T(8,128)(2,1)} %share.1), calls=%async_computation | async-start | bytes 65536 | tf_op jit(solution)/shard_map/all_to_all | solution.py:305
  16.9 29.7 %all-to-all-start.1 = ((bf16[16,32,512]{2,1,0:T(8,128)(2,1)}), bf16[16,32,512]{2,1,0:T(8,128)(2,1)S(1)}, u32[]{:S(2)}, u32[]{:S(2)}) async-start(bf16[16,32,512]{2,1,0:T(8,128)(2,1)} %merge.1), calls=%async_computation.1 | async-start | bytes 1048576 | tf_op jit(solution)/shard_map/all_to_all | solution.py:305
  80.0 41.2 %copy-start.2 = (bf16[1,32,8192]{2,1,0:T(8,128)(2,1)S(1)}, bf16[1,32,8192]{2,1,0:T(8,128)(2,1)}, u32[]{:S(2)}) copy-start(bf16[1,32,8192]{2,1,0:T(8,128)(2,1)} %local.3) | copy-start | bytes 1572868
  80.7 40.4 %copy-start = (f32[1,32,8192]{2,1,0:T(8,128)S(1)}, f32[1,32,8192]{2,1,0:T(8,128)}, u32[]{:S(2)}) copy-start(f32[1,32,8192]{2,1,0:T(8,128)} %error.3) | copy-start | bytes 3145732
  80.7 16.1 %all-to-all-start.4 = ((f32[32,4,640]{2,1,0:T(4,128)}), f32[32,4,640]{2,1,0:T(4,128)S(1)}, u32[]{:S(2)}, u32[]{:S(2)}) async-start(f32[32,4,640]{2,1,0:T(4,128)} %total.1), calls=%async_computation.4 | async-start | bytes 655360 | tf_op jit(solution)/shard_map/all_to_all | solution.py:305
  96.9 24.3 %copy-start.1 = (bf16[32,8192]{1,0:T(8,128)(2,1)S(1)}, bf16[32,8192]{1,0:T(8,128)(2,1)}, u32[]{:S(2)}) copy-start(bf16[32,8192]{1,0:T(8,128)(2,1)} %parent.3) | copy-start | bytes 1572868
  113.7 7.4 %collective-permute-start = (bf16[8,32,640]{2,1,0:T(8,128)(2,1)S(1)}, bf16[8,32,640]{2,1,0:T(8,128)(2,1)S(1)}, u32[]{:S(2)}, u32[]{:S(2)}) collective-permute-start(bf16[8,32,640]{2,1,0:T(8,128)(2,1)S(1)} %all_to_all.32.mine), channel_id=1, source_target_pairs={{0,32},{32,0},{1,33},{33,1},{2,34},{34,2},{3,35},{35,3},{4,36},{36... | collective-permute-start | bytes 983048 | tf_op jit(solution)/shard_map/ppermute | solution.py:309
